TPU v7x, 32 devices: a whole 2x2x4 slice. The times are simulated.
32 devices in a mesh: space: 16 (over z, y, x), vec: 2 (over core).
Axes of the slice: x: 2, y: 2, z: 4, core: 2. Of those that a mesh axis runs over, the one named last changes fastest.
Arguments:
- potential: float32 [16, 128, 256], P('space'), may hold values from -8.25 to 8.25
- start_basis: float32 [16, 16, 128, 256], P('vec', 'space'), may hold values from -6 to 6
Outputs:
- new_basis: float32 [16, 16, 128, 256], P('vec', 'space')
- rayleigh: float32 [16, 16], replicated
All inputs are finite; a program needn't handle non-finite values.
Results may differ from a plain program's by a relative error of at most 0.0003.
Values sent between devices are 32-bit elements; how exact they have to be, the bound alone decides.
A program may use at most 64 MiB of HBM per device.

v0:
```python
import jax
import jax.numpy as jnp
from jax import lax
from jax.sharding import PartitionSpec as P

NSWEEP = 3


SIGMA = 0.5
PREC = lax.Precision.HIGHEST


def extended(value, sides, width):
    for axis, dim in sides:
        peers, length = (lax.axis_size(axis), value.shape[dim])
        up = [(i, (i + 1) % peers) for i in range(peers)]
        down = [(j, i) for i, j in up]
        last = lax.slice_in_dim(value, length - width, length, axis=dim)
        first = lax.slice_in_dim(value, 0, width, axis=dim)
        before = lax.ppermute(last, axis, up)
        after = lax.ppermute(first, axis, down)
        value = jnp.concatenate([before, value, after], axis=dim)
    return value


def local_inner(left, right, scale):
    return jnp.einsum("kzyx,jzyx->kj", left, right, precision=PREC) * scale


def combine(coeff, vectors):
    return jnp.einsum("kj,kzyx->jzyx", coeff, vectors, precision=PREC)


def stencil(padded, potential):
    center = padded[:, 1:-1]
    beside = padded[:, 2:] + padded[:, :-2]
    beside = beside + jnp.roll(center, 1, 2) + jnp.roll(center, -1, 2)
    beside = beside + jnp.roll(center, 1, 3) + jnp.roll(center, -1, 3)
    return potential * center - beside


def inverse_factor(gram):
    lower = jnp.linalg.cholesky(gram)
    return jax.scipy.linalg.solve_triangular(
        lower, jnp.eye(gram.shape[0], dtype=jnp.float32), lower=True
    )


def local(potential, start_basis):
    mine = start_basis.shape[0]
    scale = 1.0 / (
        start_basis.shape[1] * start_basis.shape[2] * start_basis.shape[3] * lax.axis_size("space")
    )
    first = lax.axis_index("vec") * mine
    whole = lax.all_gather(start_basis, "vec", axis=0, tiled=True)
    gram = lax.psum(local_inner(whole, whole, scale), "space")
    basis_all = combine(inverse_factor(gram).T, whole)
    basis = lax.dynamic_slice_in_dim(basis_all, first, mine, 0)
    shifted = jnp.where(potential >= SIGMA, potential - SIGMA + 6.0, potential - SIGMA - 6.0)
    padded = extended(basis_all, (("space", 1),), 1)
    image_all = stencil(padded, potential)
    rayleigh = lax.psum(local_inner(basis_all, image_all, scale), "space")
    image = lax.dynamic_slice_in_dim(image_all, first, mine, 0)
    panel_mine = lax.dynamic_slice_in_dim(rayleigh, first, mine, 1)
    resid = image - combine(panel_mine, basis_all)
    correction = jnp.zeros_like(basis)
    for sweep in range(NSWEEP):
        coeff, cross = lax.psum(
            (local_inner(basis_all, correction, scale), local_inner(image_all, correction, scale)),
            "space",
        )
        padded = extended(correction, (("space", 1),), 1)
        proj = correction - combine(coeff, basis_all)
        moved = stencil(padded, potential) - combine(coeff, image_all) - SIGMA * proj
        back = cross - jnp.dot(rayleigh.T, coeff, precision=PREC)
        update = -resid - (moved - combine(back, basis_all))
        correction = correction + update / shifted
    proj_two = lax.psum(local_inner(basis_all, correction, scale), "space")
    fresh = correction - combine(proj_two, basis_all)
    fresh_all = lax.all_gather(fresh, "vec", axis=0, tiled=True)
    gram_two = lax.psum(local_inner(fresh_all, fresh_all, scale), "space")
    inverse_two = inverse_factor(gram_two)
    rows_mine = lax.dynamic_slice_in_dim(inverse_two, first, mine, 0)
    new_basis = combine(rows_mine.T, fresh_all)
    return (new_basis, rayleigh)


def solution(mesh):
    in_specs = (P("space", None, None), P("vec", "space", None, None))
    out_specs = (P("vec", "space", None, None), P())
    return jax.shard_map(local, mesh=mesh, in_specs=in_specs, out_specs=out_specs, check_vma=False)
```

profile of v0, /device:TPU:0, one launch (start us, length us, event | category | flops | bytes accessed | tf_op | source)
XLA Modules:
  0.0 550.9 jit_solution(2944374326837026506)
XLA Ops:
  7.2 2.5 copy.4
  9.8 13.3 %all-gather.3.cloned.1.call-done = f32[16,1,128,256]{2,0,3,1:T(8,128)} async-done(((f32[8,1,128,256]{2,0,3,1:T(8,128)}), f32[16,1,128,256]{2,0,3,1:T(8,128)}) %all-gather.3.cloned.1.call-update) | async-done | bytes 2097168 | tf_op jit(solution)/shard_map/all_gather | solution.py:55
  23.2 5.2 fusion.83
  28.4 42.5 %psum.70 = f32[16,16]{0,1:T(8,128)S(1)} all-reduce(f32[16,16]{0,1:T(8,128)S(1)} %fusion.83), channel_id=1, replica_groups=mesh['space'=16,'vec'=2] {'space'}, use_global_device_ids=true, to_apply=%region_0.0 | all-reduce | flops 256 | bytes 2048 | tf_op jit(solution)/shard_map/psum | solution.py:56
  70.9 1.5 cholesky.44
  72.4 0.6 compare_reduce_fusion.1
  73.1 0.6 fusion.130
  73.7 1.2 custom-call.6
  75.2 2.1 copy.7
  77.3 3.5 fusion.178
  80.9 2.0 collective-permute-start.1
  82.9 1.0 broadcast_in_dim.8
  83.9 3.7 collective-permute-start.2
  87.6 0.5 collective-permute-start.3
  88.1 0.6 concatenate.62
  88.7 0.6 concatenate.60
  89.3 2.6 fusion.102
  91.9 0.4 fusion.167
  92.3 0.5 fusion.168
  92.8 0.7 fusion.166
  93.5 36.0 %collective-permute-done = f32[16,1,128,256]{3,0,2,1:T(8,128)} collective-permute-done((f32[16,1,128,256]{3,0,2,1:T(8,128)S(1)}, f32[16,1,128,256]{3,0,2,1:T(8,128)}, u32[]{:S(2)}, u32[]{:S(2)}) %collective-permute-start) | collective-permute-done | bytes 2097184 | tf_op jit(solution)/shard_map/ppermute | solution.py:21
  129.5 52.4 %collective-permute-done.1 = f32[16,1,128,256]{3,0,2,1:T(8,128)} collective-permute-done((f32[16,1,128,256]{3,0,2,1:T(8,128)S(1)}, f32[16,1,128,256]{3,0,2,1:T(8,128)}, u32[]{:S(2)}, u32[]{:S(2)}) %collective-permute-start.1) | collective-permute-done | bytes 2097184 | tf_op jit(solution)/shard_map/ppermute | solution.py:20
  181.9 3.7 fusion.3
  185.7 3.5 fusion.87
  189.1 3.2 fusion.109
  192.3 82.5 %all-reduce.4 = (f32[16,16]{0,1:T(8,128)S(1)}, f32[16,8]{0,1:T(8,128)}, f32[16,8]{0,1:T(8,128)S(1)}) all-reduce(f32[16,16]{0,1:T(8,128)} %fusion.87, f32[16,8]{0,1:T(8,128)} %fusion.109, f32[16,8]{0,1:T(8,128)S(1)} %fusion.102), channel_id=1, replica_groups=mesh['space'=16,'vec'=2] {'space'}, use_global_device_ids=true, to_apply=%region_3.6 | all-reduce | flops 512 | bytes 4096 | tf_op jit(solution)/shard_map/psum | solution.py:62
  274.8 1.1 fusion.40
  276.1 1.1 convolution_bitcast_fusion.5
  277.5 1.2 subtract_negate_fusion
  278.7 1.0 copy-done.16
  279.8 3.1 subtract_divide_fusion
  282.9 2.6 fusion.101
  285.5 2.7 fusion.106
  288.2 2.0 collective-permute-start.5
  290.3 1.2 fusion.175
  291.4 57.7 %all-reduce.3 = (f32[16,8]{0,1:T(8,128)S(1)}, f32[16,8]{0,1:T(8,128)S(1)}) all-reduce(f32[16,8]{0,1:T(8,128)S(1)} %fusion.106, f32[16,8]{0,1:T(8,128)S(1)} %fusion.101), channel_id=1, replica_groups=mesh['space'=16,'vec'=2] {'space'}, use_global_device_ids=true, to_apply=%region_7.10 | all-reduce | flops 256 | bytes 2048 | tf_op jit(solution)/shard_map/psum | solution.py:68
  349.3 1.1 convolution_bitcast_fusion.3
  350.5 0.3 fusion.174
  350.9 1.2 fusion.38
  352.1 0.4 copy-done.2
  353.0 4.2 fusion.74
  357.2 2.6 fusion.100
  359.8 2.7 fusion.103
  362.5 13.4 %collective-permute-start.6 = (f32[8,1,128,256]{3,0,2,1:T(8,128)S(1)}, f32[8,1,128,256]{3,0,2,1:T(8,128)}, u32[]{:S(2)}, u32[]{:S(2)}) collective-permute-start(f32[8,1,128,256]{3,0,2,1:T(8,128)S(1)} %fusion.74), channel_id=1, source_target_pairs={{2,0},{4,2},{6,4},{8,6},{10,8},{12,10},{14,12},{16,14},{18,16},{20... | collective-permute-start | bytes 3145736 | tf_op jit(solution)/shard_map/ppermute | solution.py:21
  375.9 1.1 fusion.171
  377.0 52.4 %all-reduce.2 = (f32[16,8]{0,1:T(8,128)S(1)}, f32[16,8]{0,1:T(8,128)S(1)}) all-reduce(f32[16,8]{0,1:T(8,128)S(1)} %fusion.103, f32[16,8]{0,1:T(8,128)S(1)} %fusion.100), channel_id=1, replica_groups=mesh['space'=16,'vec'=2] {'space'}, use_global_device_ids=true, to_apply=%region_9.12 | all-reduce | flops 256 | bytes 2048 | tf_op jit(solution)/shard_map/psum | solution.py:68
  429.5 1.1 convolution_bitcast_fusion.1
  431.2 1.2 fusion.36
  432.4 0.4 copy-done.3
  433.3 3.9 fusion.56
  437.2 1.0 copy-done.8
  438.2 2.7 fusion.99
  440.8 36.6 %psum.78 = f32[16,8]{0,1:T(8,128)S(1)} all-reduce(f32[16,8]{0,1:T(8,128)S(1)} %fusion.99), channel_id=1, replica_groups=mesh['space'=16,'vec'=2] {'space'}, use_global_device_ids=true, to_apply=%region_10.13 | all-reduce | flops 128 | bytes 1024 | tf_op jit(solution)/shard_map/psum | solution.py:78
  477.4 3.3 fusion.34
  480.7 0.7 copy.22
  481.4 7.8 %all-gather.5.cloned.1.call-done = f32[16,1,128,256]{3,0,2,1:T(8,128)} async-done(((f32[8,1,128,256]{3,0,2,1:T(8,128)}), f32[16,1,128,256]{3,0,2,1:T(8,128)}) %all-gather.5.cloned.1.call-update) | async-done | bytes 2097168 | tf_op jit(solution)/shard_map/all_gather | solution.py:80
  489.3 5.2 fusion.84
  494.5 42.4 %psum.79 = f32[16,16]{0,1:T(8,128)S(1)} all-reduce(f32[16,16]{0,1:T(8,128)S(1)} %fusion.84), channel_id=1, replica_groups=mesh['space'=16,'vec'=2] {'space'}, use_global_device_ids=true, to_apply=%region_11.14 | all-reduce | flops 256 | bytes 2048 | tf_op jit(solution)/shard_map/psum | solution.py:81
  537.0 1.5 cholesky.55
  538.5 0.6 compare_reduce_fusion
  539.1 0.6 fusion.131
  539.8 1.2 custom-call.7
  541.2 1.1 fusion.31
  542.4 1.3 copy.21
  (69 shorter events, 3.3 us)
Async XLA Ops:
  7.2 16.0 %all-gather.3.cloned.1.call-start = ((), (), s32[]{:S(2)}) async-start(), calls=%async_computation | async-start | bytes 3145728 | tf_op jit(solution)/shard_map/all_gather | solution.py:55
  9.8 479.5 %all-gather.5.cloned.1.call-start = ((), (), s32[]{:S(2)}) async-start(), calls=%async_computation.1 | async-start | bytes 3145728 | tf_op jit(solution)/shard_map/all_gather | solution.py:80
  23.2 52.0 %copy-start.10 = (f32[16,1,128,256]{2,0,3,1:T(8,128)S(1)}, f32[16,1,128,256]{2,0,3,1:T(8,128)}, u32[]{:S(2)}) copy-start(f32[16,1,128,256]{2,0,3,1:T(8,128)} %all-gather.3.cloned.1.call-done) | copy-start | bytes 6291460
  77.3 12.0 %copy-start.11 = (f32[1,128,256]{2,1,0:T(8,128)S(1)}, f32[1,128,256]{2,1,0:T(8,128)}, u32[]{:S(2)}) copy-start(f32[1,128,256]{2,1,0:T(8,128)} %param.5) | copy-start | bytes 393220
  80.8 48.7 %collective-permute-start = (f32[16,1,128,256]{3,0,2,1:T(8,128)S(1)}, f32[16,1,128,256]{3,0,2,1:T(8,128)}, u32[]{:S(2)}, u32[]{:S(2)}) collective-permute-start(f32[16,1,128,256]{3,0,2,1:T(8,128)S(1)} %bitcast.278), channel_id=1, source_target_pairs={{2,0},{4,2},{6,4},{8,6},{10,8},{12,10},{14,12},{16,14},{18,16},{20... | collective-permute-start | bytes 6291464 | tf_op jit(solution)/shard_map/ppermute | solution.py:21
  80.9 101.1 %collective-permute-start.1 = (f32[16,1,128,256]{3,0,2,1:T(8,128)S(1)}, f32[16,1,128,256]{3,0,2,1:T(8,128)}, u32[]{:S(2)}, u32[]{:S(2)}) collective-permute-start(f32[16,1,128,256]{3,0,2,1:T(8,128)S(1)} %bitcast.279), channel_id=1, source_target_pairs={{0,2},{2,4},{4,6},{6,8},{8,10},{10,12},{12,14},{14,16},{16,18},{18... | collective-permute-start | bytes 6291464 | tf_op jit(solution)/shard_map/ppermute | solution.py:20
  83.9 194.8 %collective-permute-start.2 = (f32[8,1,128,256]{3,0,2,1:T(8,128)}, f32[8,1,128,256]{3,0,2,1:T(8,128)S(1)}, u32[]{:S(2)}, u32[]{:S(2)}) collective-permute-start(f32[8,1,128,256]{3,0,2,1:T(8,128)} %broadcast_in_dim.8), channel_id=1, source_target_pairs={{2,0},{4,2},{6,4},{8,6},{10,8},{12,10},{14,12},{16,14},{18,16},{20... | collective-permute-start | bytes 3145736 | tf_op jit(solution)/shard_map/ppermute | solution.py:21
  87.6 191.1 %collective-permute-start.3 = (f32[8,1,128,256]{3,0,2,1:T(8,128)}, f32[8,1,128,256]{3,0,2,1:T(8,128)}, u32[]{:S(2)}, u32[]{:S(2)}) collective-permute-start(f32[8,1,128,256]{3,0,2,1:T(8,128)} %broadcast_in_dim.8), channel_id=1, source_target_pairs={{0,2},{2,4},{4,6},{6,8},{8,10},{10,12},{12,14},{14,16},{16,18},{18... | collective-permute-start | bytes 3145736 | tf_op jit(solution)/shard_map/ppermute | solution.py:20
  185.6 3.5 copy-start
  274.8 1.3 copy-start.17
  275.9 1.6 copy-start.1
  277.5 2.3 copy-start.18
  277.5 2.3 copy-start.19
  278.7 4.2 copy-start.5
  278.7 1.1 copy-start.16
  282.9 68.0 %copy-start.4 = (f32[8,1,128,256]{3,0,2,1:T(8,128)}, f32[8,1,128,256]{3,0,2,1:T(8,128)S(1)}, u32[]{:S(2)}) copy-start(f32[8,1,128,256]{3,0,2,1:T(8,128)S(1)} %subtract_divide_fusion) | copy-start | bytes 3145732
  288.2 63.8 %collective-permute-start.4 = (f32[8,1,128,256]{3,0,2,1:T(8,128)S(1)}, f32[8,1,128,256]{3,0,2,1:T(8,128)}, u32[]{:S(2)}, u32[]{:S(2)}) collective-permute-start(f32[8,1,128,256]{3,0,2,1:T(8,128)S(1)} %subtract_divide_fusion), channel_id=1, source_target_pairs={{2,0},{4,2},{6,4},{8,6},{10,8},{12,10},{14,12},{16,14},{18,16},{20... | collective-permute-start | bytes 3145736 | tf_op jit(solution)/shard_map/ppermute | solution.py:21
  288.2 63.9 %collective-permute-start.5 = (f32[8,1,128,256]{3,0,2,1:T(8,128)S(1)}, f32[8,1,128,256]{3,0,2,1:T(8,128)}, u32[]{:S(2)}, u32[]{:S(2)}) collective-permute-start(f32[8,1,128,256]{3,0,2,1:T(8,128)S(1)} %subtract_divide_fusion), channel_id=1, source_target_pairs={{0,2},{2,4},{4,6},{6,8},{8,10},{10,12},{12,14},{14,16},{16,18},{18... | collective-permute-start | bytes 3145736 | tf_op jit(solution)/shard_map/ppermute | solution.py:20
  350.9 1.6 copy-start.2
  350.9 1.8 copy-start.6
  350.9 2.0 copy-start.14
  350.9 2.1 copy-start.15
  362.5 69.9 %collective-permute-start.6 = (f32[8,1,128,256]{3,0,2,1:T(8,128)S(1)}, f32[8,1,128,256]{3,0,2,1:T(8,128)}, u32[]{:S(2)}, u32[]{:S(2)}) collective-permute-start(f32[8,1,128,256]{3,0,2,1:T(8,128)S(1)} %fusion.74), channel_id=1, source_target_pairs={{2,0},{4,2},{6,4},{8,6},{10,8},{12,10},{14,12},{16,14},{18,16},{20... | collective-permute-start | bytes 3145736 | tf_op jit(solution)/shard_map/ppermute | solution.py:21
  375.9 56.5 %collective-permute-start.7 = (f32[8,1,128,256]{3,0,2,1:T(8,128)S(1)}, f32[8,1,128,256]{3,0,2,1:T(8,128)}, u32[]{:S(2)}, u32[]{:S(2)}) collective-permute-start(f32[8,1,128,256]{3,0,2,1:T(8,128)S(1)} %fusion.74), channel_id=1, source_target_pairs={{0,2},{2,4},{4,6},{6,8},{8,10},{10,12},{12,14},{14,16},{16,18},{18... | collective-permute-start | bytes 3145736 | tf_op jit(solution)/shard_map/ppermute | solution.py:20
  431.2 1.6 copy-start.3
  431.2 1.8 copy-start.7
  431.2 2.0 copy-start.12
  431.2 2.1 copy-start.13
  437.2 1.0 copy-start.8
  489.3 52.0 %copy-start.9 = (f32[16,1,128,256]{3,0,2,1:T(8,128)S(1)}, f32[16,1,128,256]{3,0,2,1:T(8,128)}, u32[]{:S(2)}) copy-start(f32[16,1,128,256]{3,0,2,1:T(8,128)} %all-gather.5.cloned.1.call-done) | copy-start | bytes 6291460
Sparse Core Ops, SparseCore 0:
  10.1 13.0 all-gather.2
  480.9 8.3 all-gather.4
where the time goes:
time: 556 us; the launch traced here: 551 us
  blocking collectives  314 us (56%)
  waiting for transfers between devices  110 us (20%)
  matrix products  60.8 us (11%)
  starting transfers between devices  21.8 us (4%)
  local copies, waits for them, and re-layouts  18.1 us (3%)
  between operations  14.9 us (3%)
  other arithmetic  11.7 us (2%)
    psum x2, blocking collectives, local(): lax.psum((local_inner(basis_all, correction, scale), local_inner(image_al...  110 us
    psum x1, blocking collectives, local(): rayleigh = lax.psum(local_inner(basis_all, image_all, scale), 'space')  82.5 us
    ppermute x4, waiting for transfers between devices, extended(): before = lax.ppermute(last, axis, up)  52.4 us
    psum x1, blocking collectives, local(): gram = lax.psum(local_inner(whole, whole, scale), 'space')  42.5 us
    psum x1, blocking collectives, local(): gram_two = lax.psum(local_inner(fresh_all, fresh_all, scale), 'space')  42.4 us
    psum x1, blocking collectives, local(): proj_two = lax.psum(local_inner(basis_all, correction, scale), 'space')  36.6 us
    ppermute x4, waiting for transfers between devices, extended(): after = lax.ppermute(first, axis, down)  36 us
    dot_general x10, matrix products, local_inner(): return jnp.einsum('kzyx,jzyx->kj', left, right, precision=PREC) * scale  32.9 us
  transfers between devices with their start and end apart: 10, of which 4 were waited for; matrix products, arithmetic and copies ran while one was open for 5% of the time, Pallas kernels for 0%

commit v1 on v0

--- a/solution.py
+++ b/solution.py
@@ -1,6 +1,10 @@
+import functools
+
 import jax
 import jax.numpy as jnp
 from jax import lax
+from jax.experimental import pallas as pl
+from jax.experimental.pallas import tpu as pltpu
 from jax.sharding import PartitionSpec as P
 
 NSWEEP = 3
@@ -85,7 +89,433 @@
     return (new_basis, rayleigh)
 
 
+MESH = pl.DeviceIdType.MESH
+F32 = jnp.float32
+BF16 = jnp.bfloat16
+NN = (((1,), (0,)), ((), ()))
+NT = (((1,), (1,)), ((), ()))
+TN = (((0,), (0,)), ((), ()))
+
+
+def small(a, b, dims=NN):
+    return lax.dot_general(a, b, dims, precision=PREC, preferred_element_type=F32)
+
+
+def split(a):
+    high = a.astype(BF16)
+    return high, (a - high.astype(F32)).astype(BF16)
+
+
+def dot3(a, b, dims=NN):
+    (ah, al), (bh, bl) = a, b
+
+    def one(p, q):
+        return lax.dot_general(p, q, dims, preferred_element_type=F32)
+
+    return one(ah, bh) + (one(ah, bl) + one(al, bh))
+
+
+def tile_of(space):
+    z, y, x = space // 4, (space // 2) % 2, space % 2
+    q = 2 * y + (x + y) % 2
+    return 4 * q + z + (q % 2) * (3 - 2 * z)
+
+
+def space_of(tile):
+    q, r = tile // 4, tile % 4
+    z = r + (q % 2) * (3 - 2 * r)
+    return z * 4 + (q // 2) * 2 + ((q + 1) // 2) % 2
+
+
+def factor_inverse(gram):
+    n = gram.shape[0]
+    rows = lax.broadcasted_iota(jnp.int32, (n, n), 0)
+    cols = lax.broadcasted_iota(jnp.int32, (n, n), 1)
+    eye = jnp.where(rows == cols, 1.0, 0.0).astype(F32)
+    upper, inv = gram, eye
+    row = lax.broadcasted_iota(jnp.int32, (n, 1), 0)
+    for k in range(n - 1):
+        mult = jnp.where(row > k, upper[:, k : k + 1] / upper[k : k + 1, k : k + 1], 0.0)
+        inv = inv - mult * inv[k : k + 1, :]
+        upper = upper - mult * upper[k : k + 1, :]
+    diag = jnp.sum(upper * eye, axis=1, keepdims=True)
+    return inv / jnp.sqrt(diag)
+
+
+def kernel(
+    nb, scale,
+    pot_in, s_in, out_ref, ray_ref,
+    pot, dinv, fs, f1, f2, ft, fq, ysend, yrecv, acc, red1, red2,
+    in_send, in_recv, pot_send, pot_recv, halo_send, halo_recv,
+    r1_send, r1_recv, r2_send, r2_recv, out_send, out_recv,
+):
+    s, v = lax.axis_index("space"), lax.axis_index("vec")
+    tile = tile_of(s)
+    half = s // 8
+    me = s * 2 + v
+    rows8 = nb * 8
+
+    barrier = pltpu.get_barrier_semaphore()
+
+    def greet(i, _):
+        peer = (me + i) % 32
+        pl.semaphore_signal(barrier, inc=1, device_id=(peer // 2, peer % 2), device_id_type=MESH)
+        return 0
+
+    lax.fori_loop(1, 32, greet, 0)
+    pl.semaphore_wait(barrier, 31)
+
+    def s_piece(dest):
+        return s_in.at[:, 0, pl.ds(pl.multiple_of(tile_of(dest) * 8, 8), 8), :]
+
+    s_slot = fs.at[1 + s % 8, pl.ds(v * 8, 8)]
+
+    def pot_piece(dest):
+        return pot_in.at[0, pl.ds(pl.multiple_of(tile_of(dest) * 8, 8), 8), :]
+
+    def s_copy(o):
+        dest = (s + o) % 16
+        return pltpu.make_async_remote_copy(
+            src_ref=s_piece(dest), dst_ref=s_slot,
+            send_sem=in_send.at[o], recv_sem=in_recv.at[s % 8, v],
+            device_id=(dest, half), device_id_type=MESH,
+        )
+
+    def pot_copy(o):
+        dest = (s + o) % 16
+        return pltpu.make_async_remote_copy(
+            src_ref=pot_piece(dest), dst_ref=pot.at[s % 8],
+            send_sem=pot_send.at[o], recv_sem=pot_recv.at[s % 8],
+            device_id=(dest, half), device_id_type=MESH,
+        )
+
+    def send_in(o, _):
+        s_copy(o).start()
+
+        @pl.when(half == v)
+        def _():
+            pot_copy(o).start()
+
+        return 0
+
+    lax.fori_loop(1, 16, send_in, 0)
+
+    @pl.when(half == v)
+    def _():
+        pltpu.make_async_copy(s_piece(s), s_slot, in_recv.at[s % 8, v]).start()
+        pltpu.make_async_copy(pot_piece(s), pot.at[s % 8], pot_recv.at[s % 8]).start()
+
+    @pl.when(half != v)
+    def _():
+        s_copy(0).start()
+
+    def done_in(z, _):
+        for w in range(2):
+            slot = fs.at[1 + z, pl.ds(w * 8, 8)]
+            pltpu.make_async_copy(slot, slot, in_recv.at[z, w]).wait()
+        pltpu.make_async_copy(pot.at[z], pot.at[z], pot_recv.at[z]).wait()
+        return 0
+
+    lax.fori_loop(0, 8, done_in, 0)
+
+    after = space_of((tile + 1) % 16)
+    before = space_of((tile + 15) % 16)
+
+    def halo(n, field):
+        def pack(z, _):
+            ysend[n, 0, z] = field[1 + z, :, 7:8, :]
+            ysend[n, 1, z] = field[1 + z, :, 0:1, :]
+            return 0
+
+        def copy(i, src, dst, device):
+            return pltpu.make_async_remote_copy(
+                src_ref=src, dst_ref=dst,
+                send_sem=halo_send.at[n, i], recv_sem=halo_recv.at[n, i],
+                device_id=device, device_id_type=MESH,
+            )
+
+        lax.fori_loop(0, 8, pack, 0)
+        copies = [
+            copy(0, ysend.at[n, 0], yrecv.at[n, 0], (after, v)),
+            copy(1, ysend.at[n, 1], yrecv.at[n, 1], (before, v)),
+            copy(2, field.at[1], field.at[9], (s, 1 - v)),
+            copy(3, field.at[8], field.at[0], (s, 1 - v)),
+        ]
+        for c in copies:
+            c.start()
+        for c in copies:
+            c.wait()
+
+    inrow = lax.broadcasted_iota(jnp.int32, (rows8, 256), 0) % 8
+    is_first, is_last = inrow == 0, inrow == 7
+
+    def flat(a):
+        return jnp.broadcast_to(a, (nb, 8, 256)).reshape(rows8, 256)
+
+    def get(field, z):
+        return field[z].reshape(rows8, 256)
+
+    def put(field, z, value):
+        field[z] = value.reshape(nb, 8, 256)
+
+    def apply_h(n, field, z):
+        mid = get(field, z + 1)
+        total = get(field, z) + get(field, z + 2)
+        total += jnp.where(is_first, flat(yrecv[n, 0, z]), pltpu.roll(mid, 1, 0))
+        total += jnp.where(is_last, flat(yrecv[n, 1, z]), pltpu.roll(mid, rows8 - 1, 0))
+        total += pltpu.roll(mid, 1, 1) + pltpu.roll(mid, 255, 1)
+        return mid, flat(pot[z][None]) * mid - total
+
+    er = lax.broadcasted_iota(jnp.int32, (rows8, nb), 0) // 8
+    ec = lax.broadcasted_iota(jnp.int32, (rows8, nb), 1)
+    expand = jnp.where(er == ec, 1.0, 0.0).astype(F32)
+    kr = lax.broadcasted_iota(jnp.int32, (rows8, rows8), 0) % 8
+    kc = lax.broadcasted_iota(jnp.int32, (rows8, rows8), 1) % 8
+    same_row = kr == kc
+
+    def kron(matrix, dims=NT):
+        wide = small(small(expand, matrix, dims), expand, NT)
+        return split(jnp.where(same_row, wide, 0.0))
+
+    def squeeze(i):
+        kept = jnp.where(same_row, acc[i], 0.0)
+        return small(small(expand, kept, TN), expand) * scale
+
+    def total_of(n, parts):
+        rank = (s % 4) * 2 + v
+        for i, part in enumerate(parts):
+            red1[n, rank, i] = part
+
+        used = len(parts)
+
+        def copy1(i):
+            peer = (rank + i) % 8
+            return pltpu.make_async_remote_copy(
+                src_ref=red1.at[n, rank, pl.ds(0, used)], dst_ref=red1.at[n, rank, pl.ds(0, used)],
+                send_sem=r1_send.at[n, i], recv_sem=r1_recv.at[n, rank],
+                device_id=((s // 4) * 4 + peer // 2, peer % 2), device_id_type=MESH,
+            )
+
+        def copy2(i):
+            peer = (s // 4 + i) % 4
+            return pltpu.make_async_remote_copy(
+                src_ref=red2.at[n, s // 4, pl.ds(0, used)], dst_ref=red2.at[n, s // 4, pl.ds(0, used)],
+                send_sem=r2_send.at[n, i], recv_sem=r2_recv.at[n, s // 4],
+                device_id=(peer * 4 + s % 4, v), device_id_type=MESH,
+            )
+
+        def stage(copy, buf, recv, mine, count):
+            for i in range(1, count):
+                copy(i).start()
+            for i in range(1, count):
+                peer = (mine + i) % count
+                slot = buf.at[n, peer, pl.ds(0, used)]
+                pltpu.make_async_copy(slot, slot, recv.at[n, peer]).wait()
+            for i in range(1, count):
+                copy(i).wait_send()
+            sums = []
+            for i in range(used):
+                total = buf[n, 0, i]
+                for p in range(1, count):
+                    total = total + buf[n, p, i]
+                sums.append(total)
+            return sums
+
+        sums = stage(copy1, red1, r1_recv, rank, 8)
+        for i, part in enumerate(sums):
+            red2[n, s // 4, i] = part
+        return stage(copy2, red2, r2_recv, s // 4, 4)
+
+    def clear(count):
+        for i in range(count):
+            acc[i] = jnp.zeros((rows8, rows8), F32)
+
+    halo(0, fs)
+    clear(5)
+
+    def first(z, _):
+        mid, image = apply_h(0, fs, z)
+        put(ft, z, image)
+        p = pot[z]
+        inverse = 1.0 / jnp.where(p >= SIGMA, p - SIGMA + 6.0, p - SIGMA - 6.0)
+        dinv[z] = inverse
+        wide = flat(inverse[None])
+        a, b = split(mid), split(image)
+        c, d = split(wide * mid), split(wide * image)
+        acc[0] += dot3(a, a, NT)
+        acc[1] += dot3(a, b, NT)
+        acc[2] += dot3(a, c, NT)
+        acc[3] += dot3(a, d, NT)
+        acc[4] += dot3(b, d, NT)
+        return 0
+
+    lax.fori_loop(0, 8, first, 0)
+    gram, raw, m0, m1, m2 = total_of(0, [squeeze(i) for i in range(5)])
+    w = factor_inverse(gram)
+
+    def conj(m):
+        return small(small(w, m), w, NT)
+
+    ray, n0, n1, n2 = conj(raw), conj(m0), conj(m1), conj(m2)
+    ray_ref[...] = ray
+    coeff = small(n0, ray) - n1
+    cross = small(n1, ray, TN) - n2
+    edge = cross - small(ray, coeff, TN) - SIGMA * coeff
+
+    kw, kray = kron(w, NN), kron(ray)
+
+    def second(z, _):
+        basis = dot3(kw, split(get(fs, z + 1)))
+        image = dot3(kw, split(get(ft, z)))
+        put(fs, z + 1, basis)
+        put(ft, z, image)
+        put(f1, z + 1, flat(dinv[z][None]) * (dot3(kray, split(basis)) - image))
+        return 0
+
+    lax.fori_loop(0, 8, second, 0)
+    halo(1, f1)
+    kco, ked = kron(coeff), kron(edge)
+
+    def third(z, _):
+        mid, image = apply_h(1, f1, z)
+        mix = dot3(kco, split(get(ft, z))) + dot3(ked, split(get(fs, z + 1)))
+        put(f2, z + 1, 2.0 * mid + flat(dinv[z][None]) * (SIGMA * mid - image + mix))
+        return 0
+
+    lax.fori_loop(0, 8, third, 0)
+    halo(2, f2)
+    clear(3)
+
+    def fourth(z, _):
+        mid, image = apply_h(2, f2, z)
+        new = mid + get(f1, z + 1) + flat(dinv[z][None]) * (SIGMA * mid - image)
+        put(fq, z, new)
+        a, b = split(get(fs, z + 1)), split(get(ft, z))
+        c, d = split(mid), split(new)
+        acc[0] += dot3(a, c, NT)
+        acc[1] += dot3(b, c, NT)
+        acc[2] += dot3(a, d, NT)
+        return 0
+
+    lax.fori_loop(0, 8, fourth, 0)
+    coeff, cross, part = total_of(1, [squeeze(i) for i in range(3)])
+    edge = cross - small(ray, coeff, TN) - SIGMA * coeff
+    proj = part + small(n1, coeff) + small(n0, edge)
+    kco, ked, kpr = kron(coeff), kron(edge), kron(proj)
+    clear(1)
+
+    def fifth(z, _):
+        basis = split(get(fs, z + 1))
+        mix = dot3(kco, split(get(ft, z))) + dot3(ked, basis)
+        fresh = get(fq, z) + flat(dinv[z][None]) * mix - dot3(kpr, basis)
+        put(fq, z, fresh)
+        a = split(fresh)
+        acc[0] += dot3(a, a, NT)
+        return 0
+
+    lax.fori_loop(0, 8, fifth, 0)
+    (gram2,) = total_of(2, [squeeze(0)])
+    kw2 = kron(factor_inverse(gram2), NN)
+
+    out_rows = out_ref.at[:, 0, pl.ds(pl.multiple_of(tile * 8, 8), 8), :]
+
+    def out_copy(z, w):
+        return pltpu.make_async_remote_copy(
+            src_ref=fq.at[z, pl.ds(w * 8, 8)], dst_ref=out_rows,
+            send_sem=out_send.at[z, w], recv_sem=out_recv.at[tile],
+            device_id=(v * 8 + z, w), device_id_type=MESH,
+        )
+
+    def last(i, _):
+        z = (tile + i) % 8
+        put(fq, z, dot3(kw2, split(get(fq, z))))
+        for w in range(2):
+            mine = (v * 8 + z) * 2 + w == me
+
+            @pl.when(mine)
+            def _():
+                pltpu.make_async_copy(
+                    fq.at[z, pl.ds(w * 8, 8)], out_rows, out_recv.at[tile]
+                ).start()
+
+            @pl.when(jnp.logical_not(mine))
+            def _():
+                out_copy(z, w).start()
+
+        return 0
+
+    lax.fori_loop(0, 8, last, 0)
+
+    def drain_in(o, _):
+        s_copy(o).wait_send()
+
+        @pl.when(half == v)
+        def _():
+            pot_copy(o).wait_send()
+
+        return 0
+
+    lax.fori_loop(1, 16, drain_in, 0)
+
+    @pl.when(half != v)
+    def _():
+        s_copy(0).wait_send()
+
+    def drain_out(z, _):
+        for w in range(2):
+            @pl.when((v * 8 + z) * 2 + w != me)
+            def _():
+                out_copy(z, w).wait_send()
+
+        return 0
+
+    lax.fori_loop(0, 8, drain_out, 0)
+
+    def done_out(t, _):
+        slot = out_ref.at[:, 0, pl.ds(pl.multiple_of(t * 8, 8), 8), :]
+        pltpu.make_async_copy(slot, slot, out_recv.at[t]).wait()
+        return 0
+
+    lax.fori_loop(0, 16, done_out, 0)
+
+
+def fused(potential, start_basis):
+    nb = start_basis.shape[0] * 2
+    sites = 16 * start_basis.shape[1] * start_basis.shape[2] * start_basis.shape[3]
+    sem = pltpu.SemaphoreType.DMA
+    field = lambda planes: pltpu.VMEM((planes, nb, 8, 256), F32)
+    return pl.pallas_call(
+        functools.partial(kernel, nb, 1.0 / sites),
+        out_shape=(
+            jax.ShapeDtypeStruct(start_basis.shape, F32),
+            jax.ShapeDtypeStruct((nb, nb), F32),
+        ),
+        in_specs=[pl.BlockSpec(memory_space=pl.ANY)] * 2,
+        out_specs=(pl.BlockSpec(memory_space=pl.ANY), pl.BlockSpec(memory_space=pltpu.VMEM)),
+        scratch_shapes=[
+            pltpu.VMEM((8, 8, 256), F32), pltpu.VMEM((8, 8, 256), F32),
+            field(10), field(10), field(10), field(8), field(8),
+            pltpu.VMEM((3, 2, 8, nb, 1, 256), F32), pltpu.VMEM((3, 2, 8, nb, 1, 256), F32),
+            pltpu.VMEM((5, nb * 8, nb * 8), F32),
+            pltpu.VMEM((3, 8, 5, nb, nb), F32), pltpu.VMEM((3, 4, 5, nb, nb), F32),
+            sem((16,)), sem((8, 2)), sem((16,)), sem((8,)), sem((3, 4)), sem((3, 4)),
+            sem((3, 8)), sem((3, 8)), sem((3, 4)), sem((3, 4)), sem((8, 2)), sem((16,)),
+        ],
+        compiler_params=pltpu.CompilerParams(
+            collective_id=0, has_side_effects=True, vmem_limit_bytes=48 * 2**20
+        ),
+        name="jacobi_davidson",
+    )(potential, start_basis)
+
+
 def solution(mesh):
     in_specs = (P("space", None, None), P("vec", "space", None, None))
     out_specs = (P("vec", "space", None, None), P())
-    return jax.shard_map(local, mesh=mesh, in_specs=in_specs, out_specs=out_specs, check_vma=False)
+
+    def body(potential, start_basis):
+        fits = mesh.shape["space"] == 16 and mesh.shape["vec"] == 2
+        if fits and start_basis.shape == (8, 1, 128, 256):
+            return fused(potential, start_basis)
+        return local(potential, start_basis)
+
+    return jax.shard_map(body, mesh=mesh, in_specs=in_specs, out_specs=out_specs, check_vma=False)

time: 556 us -> 128 us (0.23)
  blocking collectives: 314 us -> 0 us
  Pallas kernels: 0 us -> 124 us
  waiting for transfers between devices: 110 us -> 0 us
  matrix products: 60.8 us -> 0 us
  starting transfers between devices: 21.8 us -> 0 us
  local copies, waits for them, and re-layouts: 18.1 us -> 3.69 us
  between operations: 14.9 us -> 0.65 us
  other arithmetic: 11.7 us -> 0 us
    psum x6 -> x0, blocking collectives: 314 us -> none  [the longest x2 110 us: local(): lax.psum((local_inner(basis_all, correction, scale), local_inner(image_al...]
    pallas_call x0 -> x1, Pallas kernels: none -> 124 us  [fused(): pl.pallas_call(functools.partial(kernel, nb, 1.0 / sites), out_shape=(jax...]
    ppermute x8 -> x0, waiting for transfers between devices: 88.4 us -> none  [the longest x4 52.4 us: extended(): before = lax.ppermute(last, axis, up)]
    dot_general x26 -> x0, matrix products: 60.3 us -> none  [the longest x10 32.9 us: local_inner(): return jnp.einsum('kzyx,jzyx->kj', left, right, precision=PREC) * scale]
    ppermute x8 -> x0, starting transfers between devices: 21.7 us -> none  [the longest x4 17.1 us: extended(): after = lax.ppermute(first, axis, down)]
    all_gather x2 -> x0, waiting for transfers between devices: 21.2 us -> none  [the longest x1 13.3 us: local(): whole = lax.all_gather(start_basis, 'vec', axis=0, tiled=True)]
    another operation x10 -> x0, other arithmetic: 8.01 us -> none  [the longest x6 4.26 us: inverse_factor(): lower = jnp.linalg.cholesky(gram)]
  transfers between devices with their start and end apart: 10 -> 0, of which waited for: 4 -> 0; matrix products, arithmetic and copies ran while one was open for 5% -> 0% of each run, Pallas kernels for 0% -> 0%
where the time goes in v1:
time: 128 us
  Pallas kernels  124 us (97%)
  local copies, waits for them, and re-layouts  3.69 us (3%)
    pallas_call x1, Pallas kernels, fused(): pl.pallas_call(functools.partial(kernel, nb, 1.0 / sites), out_shape=(jax...  124 us
    unnamed x6, local copies, waits for them, and re-layouts  3.69 us

profile of v1, /device:TPU:0, one launch (start us, length us, event | category | flops | bytes accessed | tf_op | source)
XLA Modules:
  0.0 128.0 jit_solution(12962087027503120055)
XLA Ops:
  0.6 0.0 copy-start
  0.6 1.2 copy-done
  1.9 0.0 copy-start.1
  1.9 0.9 copy-done.1
  2.8 123.6 %jacobi_davidson.1 = (f32[8,1,128,256]{3,2,1,0:T(8,128)S(1)}, f32[16,16]{1,0:T(8,128)S(1)}) custom-call(f32[1,128,256]{2,1,0:T(8,128)S(1)} %copy-done.1, f32[8,1,128,256]{3,2,1,0:T(8,128)S(1)} %copy-done), custom_call_target="tpu_custom_call" | custom-call | tf_op jit(solution)/shard_map/jacobi_davidson/pallas_call | solution.py:487
  126.4 1.0 copy.6
  127.4 0.6 copy.7
Async XLA Ops:
  0.6 1.2 copy-start
  1.9 0.9 copy-start.1

commit v2 on v1

--- a/solution.py
+++ b/solution.py
@@ -142,11 +142,39 @@
     return inv / jnp.sqrt(diag)
 
 
+def iota(shape, dim):
+    return lax.broadcasted_iota(jnp.int32, shape, dim)
+
+
+def one_pass(a, b, dims=NN):
+    return lax.dot_general(a, b, dims, preferred_element_type=F32)
+
+
+def exact(a):
+    high, rest = a.astype(BF16), None
+    rest = a - high.astype(F32)
+    mid = rest.astype(BF16)
+    return high, mid, (rest - mid.astype(F32)).astype(BF16)
+
+
+def kron(matrix, transposed=False):
+    a, b = matrix.shape[::-1] if transposed else matrix.shape
+    rows = jnp.where(iota((8 * a, a), 0) // 8 == iota((8 * a, a), 1), 1.0, 0.0).astype(BF16)
+    cols = jnp.where(iota((b, 8 * b), 0) == iota((b, 8 * b), 1) // 8, 1.0, 0.0).astype(BF16)
+    same = iota((8 * a, 8 * b), 0) % 8 == iota((8 * a, 8 * b), 1) % 8
+
+    def one(part):
+        tall = one_pass(rows, part, NT if transposed else NN).astype(BF16)
+        return jnp.where(same, one_pass(tall, cols), 0.0).astype(BF16)
+
+    return tuple(one(part) for part in split(matrix))
+
+
 def kernel(
     nb, scale,
     pot_in, s_in, out_ref, ray_ref,
-    pot, dinv, fs, f1, f2, ft, fq, ysend, yrecv, acc, red1, red2,
-    in_send, in_recv, pot_send, pot_recv, halo_send, halo_recv,
+    pot, dinv, fs, f1, f2, ft, fq, bih, bil, ysend, yrecv, acc_s, acc, red1, red2,
+    in_send, in_recv, pot_send, pot_recv, y_sends, y_recvs, z_sends, z_recvs,
     r1_send, r1_recv, r2_send, r2_recv, out_send, out_recv,
 ):
     s, v = lax.axis_index("space"), lax.axis_index("vec")
@@ -154,6 +182,7 @@
     half = s // 8
     me = s * 2 + v
     rows8 = nb * 8
+    wide8 = 2 * rows8
 
     barrier = pltpu.get_barrier_semaphore()
 
@@ -209,44 +238,71 @@
     def _():
         s_copy(0).start()
 
-    def done_in(z, _):
-        for w in range(2):
-            slot = fs.at[1 + z, pl.ds(w * 8, 8)]
-            pltpu.make_async_copy(slot, slot, in_recv.at[z, w]).wait()
-        pltpu.make_async_copy(pot.at[z], pot.at[z], pot_recv.at[z]).wait()
-        return 0
-
-    lax.fori_loop(0, 8, done_in, 0)
 
     after = space_of((tile + 1) % 16)
     before = space_of((tile + 15) % 16)
 
-    def halo(n, field):
-        def pack(z, _):
-            ysend[n, 0, z] = field[1 + z, :, 7:8, :]
-            ysend[n, 1, z] = field[1 + z, :, 0:1, :]
+    def y_copies(n, z):
+        return [
+            pltpu.make_async_remote_copy(
+                src_ref=ysend.at[n, i, z], dst_ref=yrecv.at[n, i, z],
+                send_sem=y_sends.at[n, i, z], recv_sem=y_recvs.at[n, i, z],
+                device_id=(device, v), device_id_type=MESH,
+            )
+            for i, device in enumerate((after, before))
+        ]
+
+    def z_copy(n, field, i):
+        return pltpu.make_async_remote_copy(
+            src_ref=field.at[(8, 1)[i]], dst_ref=field.at[(0, 9)[i]],
+            send_sem=z_sends.at[n, i], recv_sem=z_recvs.at[n, i],
+            device_id=(s, 1 - v), device_id_type=MESH,
+        )
+
+    def halo_start(n, field, z):
+        ysend[n, 0, z] = field[1 + z, :, 7:8, :]
+        ysend[n, 1, z] = field[1 + z, :, 0:1, :]
+        for c in y_copies(n, z):
+            c.start()
+
+        @pl.when(z == 7)
+        def _():
+            z_copy(n, field, 0).start()
+
+        @pl.when(z == 0)
+        def _():
+            z_copy(n, field, 1).start()
+
+    def halo_wait(n, field, z):
+        for c in y_copies(n, z):
+            c.wait_recv()
+
+        @pl.when(z == 0)
+        def _():
+            z_copy(n, field, 0).wait_recv()
+
+        @pl.when(z == 7)
+        def _():
+            z_copy(n, field, 1).wait_recv()
+
+    def halo_drain(n, field):
+        def one(z, _):
+            for c in y_copies(n, z):
+                c.wait_send()
             return 0
 
-        def copy(i, src, dst, device):
-            return pltpu.make_async_remote_copy(
-                src_ref=src, dst_ref=dst,
-                send_sem=halo_send.at[n, i], recv_sem=halo_recv.at[n, i],
-                device_id=device, device_id_type=MESH,
-            )
-
-        lax.fori_loop(0, 8, pack, 0)
-        copies = [
-            copy(0, ysend.at[n, 0], yrecv.at[n, 0], (after, v)),
-            copy(1, ysend.at[n, 1], yrecv.at[n, 1], (before, v)),
-            copy(2, field.at[1], field.at[9], (s, 1 - v)),
-            copy(3, field.at[8], field.at[0], (s, 1 - v)),
-        ]
-        for c in copies:
-            c.start()
-        for c in copies:
-            c.wait()
-
-    inrow = lax.broadcasted_iota(jnp.int32, (rows8, 256), 0) % 8
+        lax.fori_loop(0, 8, one, 0)
+        z_copy(n, field, 0).wait_send()
+        z_copy(n, field, 1).wait_send()
+
+    def planes(body):
+        def step(i, _):
+            body((i + 7) % 8)
+            return 0
+
+        lax.fori_loop(0, 8, step, 0)
+
+    inrow = iota((rows8, 256), 0) % 8
     is_first, is_last = inrow == 0, inrow == 7
 
     def flat(a):
@@ -266,32 +322,23 @@
         total += pltpu.roll(mid, 1, 1) + pltpu.roll(mid, 255, 1)
         return mid, flat(pot[z][None]) * mid - total
 
-    er = lax.broadcasted_iota(jnp.int32, (rows8, nb), 0) // 8
-    ec = lax.broadcasted_iota(jnp.int32, (rows8, nb), 1)
-    expand = jnp.where(er == ec, 1.0, 0.0).astype(F32)
-    kr = lax.broadcasted_iota(jnp.int32, (rows8, rows8), 0) % 8
-    kc = lax.broadcasted_iota(jnp.int32, (rows8, rows8), 1) % 8
-    same_row = kr == kc
-
-    def kron(matrix, dims=NT):
-        wide = small(small(expand, matrix, dims), expand, NT)
-        return split(jnp.where(same_row, wide, 0.0))
-
-    def squeeze(i):
-        kept = jnp.where(same_row, acc[i], 0.0)
-        return small(small(expand, kept, TN), expand) * scale
-
-    def total_of(n, parts):
+    def squeeze(blocks):
+        width = rows8 * len(blocks)
+        wide = jnp.concatenate(blocks, axis=1)
+        wide = jnp.where(iota((rows8, width), 0) % 8 == iota((rows8, width), 1) % 8, wide, 0.0)
+        left = jnp.where(iota((nb, rows8), 0) == iota((nb, rows8), 1) // 8, 1.0, 0.0).astype(BF16)
+        right = jnp.where(iota((width, 128), 0) // 8 == iota((width, 128), 1), 1.0, 0.0).astype(BF16)
+        tall = sum(one_pass(left, part) for part in exact(wide))
+        return sum(one_pass(part, right) for part in exact(tall)) * scale
+
+    def total_of(n, blocks):
         rank = (s % 4) * 2 + v
-        for i, part in enumerate(parts):
-            red1[n, rank, i] = part
-
-        used = len(parts)
+        red1[n, rank] = squeeze(blocks)
 
         def copy1(i):
             peer = (rank + i) % 8
             return pltpu.make_async_remote_copy(
-                src_ref=red1.at[n, rank, pl.ds(0, used)], dst_ref=red1.at[n, rank, pl.ds(0, used)],
+                src_ref=red1.at[n, rank], dst_ref=red1.at[n, rank],
                 send_sem=r1_send.at[n, i], recv_sem=r1_recv.at[n, rank],
                 device_id=((s // 4) * 4 + peer // 2, peer % 2), device_id_type=MESH,
             )
@@ -299,7 +346,7 @@
         def copy2(i):
             peer = (s // 4 + i) % 4
             return pltpu.make_async_remote_copy(
-                src_ref=red2.at[n, s // 4, pl.ds(0, used)], dst_ref=red2.at[n, s // 4, pl.ds(0, used)],
+                src_ref=red2.at[n, s // 4], dst_ref=red2.at[n, s // 4],
                 send_sem=r2_send.at[n, i], recv_sem=r2_recv.at[n, s // 4],
                 device_id=(peer * 4 + s % 4, v), device_id_type=MESH,
             )
@@ -309,113 +356,119 @@
                 copy(i).start()
             for i in range(1, count):
                 peer = (mine + i) % count
-                slot = buf.at[n, peer, pl.ds(0, used)]
+                slot = buf.at[n, peer]
                 pltpu.make_async_copy(slot, slot, recv.at[n, peer]).wait()
             for i in range(1, count):
                 copy(i).wait_send()
-            sums = []
-            for i in range(used):
-                total = buf[n, 0, i]
-                for p in range(1, count):
-                    total = total + buf[n, p, i]
-                sums.append(total)
-            return sums
-
-        sums = stage(copy1, red1, r1_recv, rank, 8)
-        for i, part in enumerate(sums):
-            red2[n, s // 4, i] = part
-        return stage(copy2, red2, r2_recv, s // 4, 4)
-
-    def clear(count):
-        for i in range(count):
-            acc[i] = jnp.zeros((rows8, rows8), F32)
-
-    halo(0, fs)
-    clear(5)
-
-    def first(z, _):
-        mid, image = apply_h(0, fs, z)
-        put(ft, z, image)
+            total = buf[n, 0]
+            for p in range(1, count):
+                total = total + buf[n, p]
+            return total
+
+        red2[n, s // 4] = stage(copy1, red1, r1_recv, rank, 8)
+        total = stage(copy2, red2, r2_recv, s // 4, 4)
+        return [total[:, nb * i : nb * (i + 1)] for i in range(len(blocks))]
+
+    acc_s[...] = jnp.zeros_like(acc_s)
+    acc[...] = jnp.zeros_like(acc)
+
+    def arrive(z):
+        for w in range(2):
+            slot = fs.at[1 + z, pl.ds(w * 8, 8)]
+            pltpu.make_async_copy(slot, slot, in_recv.at[z, w]).wait()
+        pltpu.make_async_copy(pot.at[z], pot.at[z], pot_recv.at[z]).wait()
+        halo_start(0, fs, z)
         p = pot[z]
         inverse = 1.0 / jnp.where(p >= SIGMA, p - SIGMA + 6.0, p - SIGMA - 6.0)
         dinv[z] = inverse
-        wide = flat(inverse[None])
-        a, b = split(mid), split(image)
-        c, d = split(wide * mid), split(wide * image)
-        acc[0] += dot3(a, a, NT)
-        acc[1] += dot3(a, b, NT)
-        acc[2] += dot3(a, c, NT)
-        acc[3] += dot3(a, d, NT)
-        acc[4] += dot3(b, d, NT)
-        return 0
-
-    lax.fori_loop(0, 8, first, 0)
-    gram, raw, m0, m1, m2 = total_of(0, [squeeze(i) for i in range(5)])
+        mid = get(fs, z + 1)
+        both = jnp.concatenate([mid, flat(inverse[None]) * mid], axis=0)
+        acc_s[...] += dot3(split(mid), split(both), NT)
+
+    planes(arrive)
+
+    def first(z):
+        halo_wait(0, fs, z)
+        mid, image = apply_h(0, fs, z)
+        put(ft, z, image)
+        left = jnp.concatenate([mid, image], axis=0)
+        right = jnp.concatenate([image, flat(dinv[z][None]) * image], axis=0)
+        acc[...] += dot3(split(left), split(right), NT)
+
+    planes(first)
+    lo, hi = slice(0, rows8), slice(rows8, wide8)
+    gram, m0, raw, m1, m2 = total_of(
+        0, [acc_s[:, lo], acc_s[:, hi], acc[lo, lo], acc[lo, hi], acc[hi, hi]]
+    )
     w = factor_inverse(gram)
 
     def conj(m):
         return small(small(w, m), w, NT)
 
-    ray, n0, n1, n2 = conj(raw), conj(m0), conj(m1), conj(m2)
+    def side(*parts):
+        return jnp.concatenate(parts, axis=1)
+
+    def stack(*parts):
+        return jnp.concatenate(parts, axis=0)
+
+    ray = conj(raw)
+    zero = jnp.zeros_like(w)
+    kbig = kron(stack(side(w, zero), side(zero, w), side(small(ray, w, TN), -w)))
+
+    def second(z):
+        mixed = dot3(kbig, split(stack(get(fs, z + 1), get(ft, z))))
+        basis, image, resid = mixed[lo], mixed[hi], mixed[wide8:]
+        put(f1, z + 1, flat(dinv[z][None]) * resid)
+        halo_start(1, f1, z)
+        high, low = split(stack(image, basis))
+        bih[z] = high
+        bil[z] = low
+
+    planes(second)
     ray_ref[...] = ray
+    n0, n1, n2 = conj(m0), conj(m1), conj(m2)
     coeff = small(n0, ray) - n1
     cross = small(n1, ray, TN) - n2
     edge = cross - small(ray, coeff, TN) - SIGMA * coeff
-
-    kw, kray = kron(w, NN), kron(ray)
-
-    def second(z, _):
-        basis = dot3(kw, split(get(fs, z + 1)))
-        image = dot3(kw, split(get(ft, z)))
-        put(fs, z + 1, basis)
-        put(ft, z, image)
-        put(f1, z + 1, flat(dinv[z][None]) * (dot3(kray, split(basis)) - image))
-        return 0
-
-    lax.fori_loop(0, 8, second, 0)
-    halo(1, f1)
-    kco, ked = kron(coeff), kron(edge)
-
-    def third(z, _):
+    kmix = kron(stack(coeff, edge), True)
+
+    def third(z):
+        halo_wait(1, f1, z)
         mid, image = apply_h(1, f1, z)
-        mix = dot3(kco, split(get(ft, z))) + dot3(ked, split(get(fs, z + 1)))
+        mix = dot3(kmix, (bih[z], bil[z]))
         put(f2, z + 1, 2.0 * mid + flat(dinv[z][None]) * (SIGMA * mid - image + mix))
-        return 0
-
-    lax.fori_loop(0, 8, third, 0)
-    halo(2, f2)
-    clear(3)
-
-    def fourth(z, _):
+        halo_start(2, f2, z)
+
+    planes(third)
+    acc[...] = jnp.zeros_like(acc)
+
+    def fourth(z):
+        halo_wait(2, f2, z)
         mid, image = apply_h(2, f2, z)
         new = mid + get(f1, z + 1) + flat(dinv[z][None]) * (SIGMA * mid - image)
         put(fq, z, new)
-        a, b = split(get(fs, z + 1)), split(get(ft, z))
-        c, d = split(mid), split(new)
-        acc[0] += dot3(a, c, NT)
-        acc[1] += dot3(b, c, NT)
-        acc[2] += dot3(a, d, NT)
-        return 0
-
-    lax.fori_loop(0, 8, fourth, 0)
-    coeff, cross, part = total_of(1, [squeeze(i) for i in range(3)])
+        acc[...] += dot3((bih[z], bil[z]), split(stack(mid, new)), NT)
+
+    planes(fourth)
+    cross, coeff, part = total_of(1, [acc[lo, lo], acc[hi, lo], acc[hi, hi]])
     edge = cross - small(ray, coeff, TN) - SIGMA * coeff
     proj = part + small(n1, coeff) + small(n0, edge)
-    kco, ked, kpr = kron(coeff), kron(edge), kron(proj)
-    clear(1)
-
-    def fifth(z, _):
-        basis = split(get(fs, z + 1))
-        mix = dot3(kco, split(get(ft, z))) + dot3(ked, basis)
-        fresh = get(fq, z) + flat(dinv[z][None]) * mix - dot3(kpr, basis)
+    klast = kron(stack(side(coeff, zero), side(edge, proj)), True)
+    acc_s[...] = jnp.zeros_like(acc_s)
+
+    def fifth(z):
+        mixed = dot3(klast, (bih[z], bil[z]))
+        fresh = get(fq, z) + flat(dinv[z][None]) * mixed[lo] - mixed[hi]
         put(fq, z, fresh)
         a = split(fresh)
-        acc[0] += dot3(a, a, NT)
-        return 0
-
-    lax.fori_loop(0, 8, fifth, 0)
-    (gram2,) = total_of(2, [squeeze(0)])
-    kw2 = kron(factor_inverse(gram2), NN)
+        acc_s[:, lo] += dot3(a, a, NT)
+
+    planes(fifth)
+    (gram2,) = total_of(2, [acc_s[:, lo]])
+    kw2 = kron(factor_inverse(gram2))
+    halo_drain(0, fs)
+    halo_drain(1, f1)
+    halo_drain(2, f2)
 
     out_rows = out_ref.at[:, 0, pl.ds(pl.multiple_of(tile * 8, 8), 8), :]
 
@@ -495,10 +548,12 @@
         scratch_shapes=[
             pltpu.VMEM((8, 8, 256), F32), pltpu.VMEM((8, 8, 256), F32),
             field(10), field(10), field(10), field(8), field(8),
+            pltpu.VMEM((8, nb * 16, 256), BF16), pltpu.VMEM((8, nb * 16, 256), BF16),
             pltpu.VMEM((3, 2, 8, nb, 1, 256), F32), pltpu.VMEM((3, 2, 8, nb, 1, 256), F32),
-            pltpu.VMEM((5, nb * 8, nb * 8), F32),
-            pltpu.VMEM((3, 8, 5, nb, nb), F32), pltpu.VMEM((3, 4, 5, nb, nb), F32),
-            sem((16,)), sem((8, 2)), sem((16,)), sem((8,)), sem((3, 4)), sem((3, 4)),
+            pltpu.VMEM((nb * 8, nb * 16), F32), pltpu.VMEM((nb * 16, nb * 16), F32),
+            pltpu.VMEM((3, 8, nb, 128), F32), pltpu.VMEM((3, 4, nb, 128), F32),
+            sem((16,)), sem((8, 2)), sem((16,)), sem((8,)),
+            sem((3, 2, 8)), sem((3, 2, 8)), sem((3, 2)), sem((3, 2)),
             sem((3, 8)), sem((3, 8)), sem((3, 4)), sem((3, 4)), sem((8, 2)), sem((16,)),
         ],
         compiler_params=pltpu.CompilerParams(

time: 128 us -> 112 us (0.88)
  Pallas kernels: 124 us -> 107 us
    pallas_call x1, Pallas kernels: 124 us -> 107 us  [fused(): pl.pallas_call(functools.partial(kernel, nb, 1.0 / sites), out_shape=(jax...]
where the time goes in v2:
time: 112 us; the launch traced here: 111 us
  Pallas kernels  107 us (96%)
  local copies, waits for them, and re-layouts  3.69 us (3%)
    pallas_call x1, Pallas kernels, fused(): pl.pallas_call(functools.partial(kernel, nb, 1.0 / sites), out_shape=(jax...  107 us
    unnamed x6, local copies, waits for them, and re-layouts  3.69 us

profile of v2, /device:TPU:0, one launch (start us, length us, event | category | flops | bytes accessed | tf_op | source)
XLA Modules:
  0.0 111.3 jit_solution(4219830238376684901)
XLA Ops:
  0.6 0.0 copy-start
  0.6 1.2 %copy-done = f32[8,1,128,256]{3,2,1,0:T(8,128)S(1)} copy-done((f32[8,1,128,256]{3,2,1,0:T(8,128)S(1)}, f32[8,1,128,256]{3,2,1,0:T(8,128)}, u32[]{:S(2)}) %copy-start) | copy-done | bytes 1048600
  1.9 0.0 copy-start.1
  1.9 0.9 copy-done.1
  2.8 106.9 %jacobi_davidson.1 = (f32[8,1,128,256]{3,2,1,0:T(8,128)S(1)}, f32[16,16]{1,0:T(8,128)S(1)}) custom-call(f32[1,128,256]{2,1,0:T(8,128)S(1)} %copy-done.1, f32[8,1,128,256]{3,2,1,0:T(8,128)S(1)} %copy-done), custom_call_target="tpu_custom_call" | custom-call | tf_op jit(solution)/shard_map/jacobi_davidson/pallas_call | solution.py:540
  109.7 1.0 copy.6
  110.7 0.6 copy.7
Async XLA Ops:
  0.6 1.2 %copy-start = (f32[8,1,128,256]{3,2,1,0:T(8,128)S(1)}, f32[8,1,128,256]{3,2,1,0:T(8,128)}, u32[]{:S(2)}) copy-start(f32[8,1,128,256]{3,2,1,0:T(8,128)} %s_in.1) | copy-start | bytes 3145732
  1.9 0.9 copy-start.1

commit v3 on v2

--- a/solution.py
+++ b/solution.py
@@ -173,9 +173,9 @@
 def kernel(
     nb, scale,
     pot_in, s_in, out_ref, ray_ref,
-    pot, dinv, fs, f1, f2, ft, fq, bih, bil, ysend, yrecv, acc_s, acc, red1, red2,
+    pot, dinv, fs, f1, f2, ft, fq, bih, bil, ysend, yrecv, acc_s, acc, red1, red2, home,
     in_send, in_recv, pot_send, pot_recv, y_sends, y_recvs, z_sends, z_recvs,
-    r1_send, r1_recv, r2_send, r2_recv, out_send, out_recv,
+    r1_send, r1_recv, r2_send, r2_recv, out_send, out_recv, fwd_send, fwd_recv,
 ):
     s, v = lax.axis_index("space"), lax.axis_index("vec")
     tile = tile_of(s)
@@ -456,48 +456,80 @@
     klast = kron(stack(side(coeff, zero), side(edge, proj)), True)
     acc_s[...] = jnp.zeros_like(acc_s)
 
-    def fifth(z):
+    @pl.when(v == 0)
+    def _():
+        for i in range(16):
+            home[i, 8:16] = jnp.zeros((8, 8, 256), F32)
+
+    def out_copy(z, w):
+        return pltpu.make_async_remote_copy(
+            src_ref=fq.at[z, pl.ds(w * 8, 8)], dst_ref=home.at[tile, pl.ds(w * 8, 8)],
+            send_sem=out_send.at[z, w], recv_sem=out_recv.at[tile],
+            device_id=(v * 8 + z, w), device_id_type=MESH,
+        )
+
+    def send_out(z):
+        for w in range(2):
+            mine = (v * 8 + z) * 2 + w == me
+
+            @pl.when(mine)
+            def _():
+                pltpu.make_async_copy(
+                    fq.at[z, pl.ds(w * 8, 8)], home.at[tile, pl.ds(w * 8, 8)], out_recv.at[tile]
+                ).start()
+
+            @pl.when(jnp.logical_not(mine))
+            def _():
+                out_copy(z, w).start()
+
+    def fifth(i, _):
+        z = (tile + i) % 8
         mixed = dot3(klast, (bih[z], bil[z]))
         fresh = get(fq, z) + flat(dinv[z][None]) * mixed[lo] - mixed[hi]
         put(fq, z, fresh)
+        send_out(z)
         a = split(fresh)
         acc_s[:, lo] += dot3(a, a, NT)
-
-    planes(fifth)
+        return 0
+
+    lax.fori_loop(0, 8, fifth, 0)
     (gram2,) = total_of(2, [acc_s[:, lo]])
-    kw2 = kron(factor_inverse(gram2))
-    halo_drain(0, fs)
-    halo_drain(1, f1)
-    halo_drain(2, f2)
-
-    out_rows = out_ref.at[:, 0, pl.ds(pl.multiple_of(tile * 8, 8), 8), :]
-
-    def out_copy(z, w):
+    w2 = factor_inverse(gram2)
+    kw2 = kron(jnp.where(v == 0, w2[0:8], w2[8:16]))
+    def forward(j):
         return pltpu.make_async_remote_copy(
-            src_ref=fq.at[z, pl.ds(w * 8, 8)], dst_ref=out_rows,
-            send_sem=out_send.at[z, w], recv_sem=out_recv.at[tile],
-            device_id=(v * 8 + z, w), device_id_type=MESH,
+            src_ref=home.at[j, pl.ds(0, 8)], dst_ref=home.at[j, pl.ds(0, 8)],
+            send_sem=fwd_send.at[j], recv_sem=fwd_recv.at[j],
+            device_id=(s, 1), device_id_type=MESH,
         )
 
     def last(i, _):
-        z = (tile + i) % 8
-        put(fq, z, dot3(kw2, split(get(fq, z))))
-        for w in range(2):
-            mine = (v * 8 + z) * 2 + w == me
-
-            @pl.when(mine)
-            def _():
-                pltpu.make_async_copy(
-                    fq.at[z, pl.ds(w * 8, 8)], out_rows, out_recv.at[tile]
-                ).start()
-
-            @pl.when(jnp.logical_not(mine))
-            def _():
-                out_copy(z, w).start()
-
+        j = (s + 32 - i // 2 - 8 * (i % 2)) % 16
+        slot = home.at[j, pl.ds(v * 8, 8)]
+        pltpu.make_async_copy(slot, slot, out_recv.at[j]).wait()
+
+        @pl.when(v == 0)
+        def _():
+            forward(j).start()
+
+        @pl.when(v == 1)
+        def _():
+            low = home.at[j, pl.ds(0, 8)]
+            pltpu.make_async_copy(low, low, fwd_recv.at[j]).wait()
+
+        done = dot3(kw2, split(home[j].reshape(rows8, 256)))
+        out_ref[:, 0, pl.ds(pl.multiple_of(j * 8, 8), 8), :] = done.reshape(8, 8, 256)
         return 0
 
-    lax.fori_loop(0, 8, last, 0)
+    lax.fori_loop(0, 16, last, 0)
+
+    @pl.when(v == 0)
+    def _():
+        def drain(j, _):
+            forward(j).wait_send()
+            return 0
+
+        lax.fori_loop(0, 16, drain, 0)
 
     def drain_in(o, _):
         s_copy(o).wait_send()
@@ -523,13 +555,9 @@
         return 0
 
     lax.fori_loop(0, 8, drain_out, 0)
-
-    def done_out(t, _):
-        slot = out_ref.at[:, 0, pl.ds(pl.multiple_of(t * 8, 8), 8), :]
-        pltpu.make_async_copy(slot, slot, out_recv.at[t]).wait()
-        return 0
-
-    lax.fori_loop(0, 16, done_out, 0)
+    halo_drain(0, fs)
+    halo_drain(1, f1)
+    halo_drain(2, f2)
 
 
 def fused(potential, start_basis):
@@ -544,17 +572,18 @@
             jax.ShapeDtypeStruct((nb, nb), F32),
         ),
         in_specs=[pl.BlockSpec(memory_space=pl.ANY)] * 2,
-        out_specs=(pl.BlockSpec(memory_space=pl.ANY), pl.BlockSpec(memory_space=pltpu.VMEM)),
+        out_specs=(pl.BlockSpec(memory_space=pltpu.VMEM), pl.BlockSpec(memory_space=pltpu.VMEM)),
         scratch_shapes=[
             pltpu.VMEM((8, 8, 256), F32), pltpu.VMEM((8, 8, 256), F32),
             field(10), field(10), field(10), field(8), field(8),
             pltpu.VMEM((8, nb * 16, 256), BF16), pltpu.VMEM((8, nb * 16, 256), BF16),
             pltpu.VMEM((3, 2, 8, nb, 1, 256), F32), pltpu.VMEM((3, 2, 8, nb, 1, 256), F32),
             pltpu.VMEM((nb * 8, nb * 16), F32), pltpu.VMEM((nb * 16, nb * 16), F32),
-            pltpu.VMEM((3, 8, nb, 128), F32), pltpu.VMEM((3, 4, nb, 128), F32),
+            pltpu.VMEM((3, 8, nb, 128), F32), pltpu.VMEM((3, 4, nb, 128), F32), field(16),
             sem((16,)), sem((8, 2)), sem((16,)), sem((8,)),
             sem((3, 2, 8)), sem((3, 2, 8)), sem((3, 2)), sem((3, 2)),
             sem((3, 8)), sem((3, 8)), sem((3, 4)), sem((3, 4)), sem((8, 2)), sem((16,)),
+            sem((16,)), sem((16,)),
         ],
         compiler_params=pltpu.CompilerParams(
             collective_id=0, has_side_effects=True, vmem_limit_bytes=48 * 2**20

time: 112 us -> 106 us (0.946)
  Pallas kernels: 107 us -> 102 us
    pallas_call x1, Pallas kernels: 107 us -> 102 us  [fused(): pl.pallas_call(functools.partial(kernel, nb, 1.0 / sites), out_shape=(jax...]
where the time goes in v3:
time: 106 us
  Pallas kernels  102 us (96%)
  local copies, waits for them, and re-layouts  3.69 us (3%)
    pallas_call x1, Pallas kernels, fused(): pl.pallas_call(functools.partial(kernel, nb, 1.0 / sites), out_shape=(jax...  102 us
    unnamed x6, local copies, waits for them, and re-layouts  3.69 us

profile of v3, /device:TPU:0, one launch (start us, length us, event | category | flops | bytes accessed | tf_op | source)
XLA Modules:
  0.0 105.9 jit_solution(812893745653898478)
XLA Ops:
  0.6 0.0 copy-start
  0.6 1.2 %copy-done = f32[8,1,128,256]{3,2,1,0:T(8,128)S(1)} copy-done((f32[8,1,128,256]{3,2,1,0:T(8,128)S(1)}, f32[8,1,128,256]{3,2,1,0:T(8,128)}, u32[]{:S(2)}) %copy-start) | copy-done | bytes 1048600
  1.9 0.0 copy-start.1
  1.9 0.9 copy-done.1
  2.8 101.6 %jacobi_davidson.1 = (f32[8,1,128,256]{3,2,1,0:T(8,128)S(1)}, f32[16,16]{1,0:T(8,128)S(1)}) custom-call(f32[1,128,256]{2,1,0:T(8,128)S(1)} %copy-done.1, f32[8,1,128,256]{3,2,1,0:T(8,128)S(1)} %copy-done), custom_call_target="tpu_custom_call" | custom-call | tf_op jit(solution)/shard_map/jacobi_davidson/pallas_call | solution.py:568
  104.3 1.0 copy.6
  105.3 0.6 copy.7
Async XLA Ops:
  0.6 1.2 %copy-start = (f32[8,1,128,256]{3,2,1,0:T(8,128)S(1)}, f32[8,1,128,256]{3,2,1,0:T(8,128)}, u32[]{:S(2)}) copy-start(f32[8,1,128,256]{3,2,1,0:T(8,128)} %s_in.1) | copy-start | bytes 3145732
  1.9 0.9 copy-start.1

commit v4 on v3

--- a/solution.py
+++ b/solution.py
@@ -300,7 +300,7 @@
             body((i + 7) % 8)
             return 0
 
-        lax.fori_loop(0, 8, step, 0)
+        lax.fori_loop(0, 8, step, 0, unroll=2)
 
     inrow = iota((rows8, 256), 0) % 8
     is_first, is_last = inrow == 0, inrow == 7
@@ -492,7 +492,7 @@
         acc_s[:, lo] += dot3(a, a, NT)
         return 0
 
-    lax.fori_loop(0, 8, fifth, 0)
+    lax.fori_loop(0, 8, fifth, 0, unroll=2)
     (gram2,) = total_of(2, [acc_s[:, lo]])
     w2 = factor_inverse(gram2)
     kw2 = kron(jnp.where(v == 0, w2[0:8], w2[8:16]))
@@ -521,7 +521,7 @@
         out_ref[:, 0, pl.ds(pl.multiple_of(j * 8, 8), 8), :] = done.reshape(8, 8, 256)
         return 0
 
-    lax.fori_loop(0, 16, last, 0)
+    lax.fori_loop(0, 16, last, 0, unroll=2)
 
     @pl.when(v == 0)
     def _():

time: 106 us -> 109 us (1.028)
  Pallas kernels: 102 us -> 104 us
    pallas_call x1, Pallas kernels: 102 us -> 104 us  [fused(): pl.pallas_call(functools.partial(kernel, nb, 1.0 / sites), out_shape=(jax...]
where the time goes in v4:
time: 109 us; the launch traced here: 108 us
  Pallas kernels  104 us (95%)
  local copies, waits for them, and re-layouts  3.69 us (3%)
    pallas_call x1, Pallas kernels, fused(): pl.pallas_call(functools.partial(kernel, nb, 1.0 / sites), out_shape=(jax...  104 us
    unnamed x6, local copies, waits for them, and re-layouts  3.69 us

profile of v4, /device:TPU:0, one launch (start us, length us, event | category | flops | bytes accessed | tf_op | source)
XLA Modules:
  0.0 108.3 jit_solution(3483617479018525730)
XLA Ops:
  0.6 0.0 copy-start
  0.6 1.2 %copy-done = f32[8,1,128,256]{3,2,1,0:T(8,128)S(1)} copy-done((f32[8,1,128,256]{3,2,1,0:T(8,128)S(1)}, f32[8,1,128,256]{3,2,1,0:T(8,128)}, u32[]{:S(2)}) %copy-start) | copy-done | bytes 1048600
  1.9 0.0 copy-start.1
  1.9 0.9 copy-done.1
  2.8 104.0 %jacobi_davidson.1 = (f32[8,1,128,256]{3,2,1,0:T(8,128)S(1)}, f32[16,16]{1,0:T(8,128)S(1)}) custom-call(f32[1,128,256]{2,1,0:T(8,128)S(1)} %copy-done.1, f32[8,1,128,256]{3,2,1,0:T(8,128)S(1)} %copy-done), custom_call_target="tpu_custom_call" | custom-call | tf_op jit(solution)/shard_map/jacobi_davidson/pallas_call | solution.py:568
  106.7 1.0 copy.6
  107.7 0.6 copy.7
Async XLA Ops:
  0.6 1.2 %copy-start = (f32[8,1,128,256]{3,2,1,0:T(8,128)S(1)}, f32[8,1,128,256]{3,2,1,0:T(8,128)}, u32[]{:S(2)}) copy-start(f32[8,1,128,256]{3,2,1,0:T(8,128)} %s_in.1) | copy-start | bytes 3145732
  1.9 0.9 copy-start.1
